TPU v7x, 256 devices: a whole 4x4x8 slice. The times are simulated.
256 devices in a mesh: gx: 8 (over x, core), gy: 32 (over z, y).
Axes of the slice: x: 4, y: 4, z: 8, core: 2. Of those that a mesh axis runs over, the one named last changes fastest.
Arguments:
- prompt_tokens: bfloat16 [512, 18432], P(None, ('gx', 'gy')), may hold values from -6 to 6
- decode_tokens: bfloat16 [4, 128, 18432], P(None, None, ('gx', 'gy')), may hold values from -6 to 6
- gate_weight: bfloat16 [18432, 36864], P('gx', 'gy'), may hold values from -0.046875 to 0.046875
- up_weight: bfloat16 [18432, 36864], P('gx', 'gy'), may hold values from -0.046875 to 0.046875
Outputs:
- prompt_hidden: bfloat16 [512, 36864], P('gx', 'gy')
- decode_hidden: bfloat16 [4, 128, 36864], P(None, 'gx', 'gy')
All inputs are finite; a program needn't handle non-finite values.
Results may differ from a plain program's by a relative error of at most 0.025.
Values may be sent and summed in bfloat16 or wider, within the bound.
A program may use at most 64 MiB of HBM per device.

v0:
```python
import jax
import jax.numpy as jnp
from jax import lax
from jax.sharding import PartitionSpec as P


def both_terms(rows_in, gate_weight, up_weight):
    gate_part = jnp.dot(rows_in, gate_weight, preferred_element_type=jnp.float32)
    up_part = jnp.dot(rows_in, up_weight, preferred_element_type=jnp.float32)
    return jnp.concatenate([gate_part, up_part], axis=-1)


def make_terms(gathered, gate_weight, up_weight):
    return both_terms(gathered, gate_weight, up_weight)


def activate(summed, columns):
    gate_sum = summed[..., :columns]
    up_sum = summed[..., columns:]
    return (jax.nn.silu(gate_sum) * up_sum).astype(jnp.bfloat16)


def shards(prompt_tokens, decode_tokens, gate_weight, up_weight):
    columns = gate_weight.shape[1]
    gathered = lax.all_gather(prompt_tokens, "gy", axis=1, tiled=True)
    prompt_sum = lax.psum_scatter(
        make_terms(gathered, gate_weight, up_weight).astype(jnp.bfloat16),
        "gx",
        scatter_dimension=0,
        tiled=True,
    ).astype(jnp.float32)
    results = []
    for step_index in range(decode_tokens.shape[0]):
        current = lax.all_gather(decode_tokens[step_index], "gy", axis=1, tiled=True)
        summed = lax.psum_scatter(
            make_terms(current, gate_weight, up_weight).astype(jnp.bfloat16),
            "gx",
            scatter_dimension=0,
            tiled=True,
        ).astype(jnp.float32)
        results.append(activate(summed, columns))
    return (activate(prompt_sum, columns), jnp.stack(results, 0))


def solution(mesh):
    in_specs = (P(None, ("gx", "gy")), P(None, None, ("gx", "gy")), P("gx", "gy"), P("gx", "gy"))
    out_specs = (P("gx", "gy"), P(None, "gx", "gy"))
    return jax.shard_map(shards, mesh=mesh, in_specs=in_specs, out_specs=out_specs, check_vma=False)
```

profile of v0, /device:TPU:1, one launch (start us, length us, event | category | flops | bytes accessed | tf_op | source)
XLA Modules:
  0.0 313.2 jit_solution(1542397881932612054)
XLA Ops:
  8.0 0.7 all-gather.6.cloned.1.call-update
  8.8 0.9 fusion.17
  9.7 43.8 %all-gather.3 = bf16[1,128,2304]{1,2,0:T(8,128)(2,1)S(1)} all-gather(bf16[1,128,72]{1,2,0:T(8,128)(2,1)S(1)} %get-tuple-element.4), channel_id=5, replica_groups=mesh['gx'=8,'gy'=32] {'gy'}, dimensions={2}, use_global_device_ids=true | all-gather | bytes 608256 | tf_op jit(solution)/shard_map/all_gather | solution.py:34
  53.5 3.5 %convolution_convert_fusion.2 = bf16[128,1152]{1,0:T(8,128)(2,1)S(1)} fusion(bf16[2304,1152]{1,0:T(8,128)(2,1)} %param.7, bf16[1,128,2304]{1,2,0:T(8,128)(2,1)S(1)} %all-gather.3), kind=kOutput, calls=%fused_computation.2 | convolution fusion | flops 679624704 | bytes 6193152 | tf_op jit(solution)/shard_map/dot_general | solution.py:9
  57.0 1.0 convolution_convert_fusion.3
  58.0 0.9 pad_maximum_fusion.4
  58.9 0.0 reduce-scatter.12.cloned.1.call-start
  58.9 39.2 %all-gather.2 = bf16[1,128,2304]{1,2,0:T(8,128)(2,1)S(1)} all-gather(bf16[1,128,72]{1,2,0:T(8,128)(2,1)S(1)} %get-tuple-element.5), channel_id=4, replica_groups=mesh['gx'=8,'gy'=32] {'gy'}, dimensions={2}, use_global_device_ids=true | all-gather | bytes 608256 | tf_op jit(solution)/shard_map/all_gather | solution.py:34
  98.1 3.5 %convolution_convert_fusion.4 = bf16[128,1152]{1,0:T(8,128)(2,1)S(1)} fusion(bf16[2304,1152]{1,0:T(8,128)(2,1)} %param.7, bf16[1,128,2304]{1,2,0:T(8,128)(2,1)S(1)} %all-gather.2), kind=kOutput, calls=%fused_computation.4 | convolution fusion | flops 679624704 | bytes 6193152 | tf_op jit(solution)/shard_map/dot_general | solution.py:9
  101.6 3.5 %convolution_convert_fusion.5 = bf16[128,1152]{1,0:T(8,128)(2,1)S(1)} fusion(bf16[2304,1152]{1,0:T(8,128)(2,1)} %param.6, bf16[1,128,2304]{1,2,0:T(8,128)(2,1)S(1)} %all-gather.2), kind=kOutput, calls=%fused_computation.5 | convolution fusion | flops 679624704 | bytes 6193152 | tf_op jit(solution)/shard_map/dot_general | solution.py:8
  105.1 0.9 pad_maximum_fusion.3
  106.0 36.3 %all-gather.1 = bf16[1,128,2304]{1,2,0:T(8,128)(2,1)S(1)} all-gather(bf16[1,128,72]{1,2,0:T(8,128)(2,1)S(1)} %get-tuple-element.3), channel_id=3, replica_groups=mesh['gx'=8,'gy'=32] {'gy'}, dimensions={2}, use_global_device_ids=true | all-gather | bytes 608256 | tf_op jit(solution)/shard_map/all_gather | solution.py:34
  142.3 3.5 %convolution_convert_fusion.6 = bf16[128,1152]{1,0:T(8,128)(2,1)S(1)} fusion(bf16[2304,1152]{1,0:T(8,128)(2,1)} %param.7, bf16[1,128,2304]{1,2,0:T(8,128)(2,1)S(1)} %all-gather.1), kind=kOutput, calls=%fused_computation.6 | convolution fusion | flops 679624704 | bytes 6193152 | tf_op jit(solution)/shard_map/dot_general | solution.py:9
  145.8 3.5 %convolution_convert_fusion.7 = bf16[128,1152]{1,0:T(8,128)(2,1)S(1)} fusion(bf16[2304,1152]{1,0:T(8,128)(2,1)} %param.6, bf16[1,128,2304]{1,2,0:T(8,128)(2,1)S(1)} %all-gather.1), kind=kOutput, calls=%fused_computation.7 | convolution fusion | flops 679624704 | bytes 6193152 | tf_op jit(solution)/shard_map/dot_general | solution.py:8
  149.3 0.9 pad_maximum_fusion.2
  150.2 35.9 %all-gather = bf16[1,128,2304]{1,2,0:T(8,128)(2,1)S(1)} all-gather(bf16[1,128,72]{1,2,0:T(8,128)(2,1)S(1)} %get-tuple-element.2), channel_id=2, replica_groups=mesh['gx'=8,'gy'=32] {'gy'}, dimensions={2}, use_global_device_ids=true | all-gather | bytes 608256 | tf_op jit(solution)/shard_map/all_gather | solution.py:34
  186.1 3.5 %convolution_convert_fusion.8 = bf16[128,1152]{1,0:T(8,128)(2,1)S(1)} fusion(bf16[2304,1152]{1,0:T(8,128)(2,1)} %param.7, bf16[1,128,2304]{1,2,0:T(8,128)(2,1)S(1)} %all-gather), kind=kOutput, calls=%fused_computation.8 | convolution fusion | flops 679624704 | bytes 6193152 | tf_op jit(solution)/shard_map/dot_general | solution.py:9
  189.6 3.5 %convolution_convert_fusion.9 = bf16[128,1152]{1,0:T(8,128)(2,1)S(1)} fusion(bf16[2304,1152]{1,0:T(8,128)(2,1)} %param.6, bf16[1,128,2304]{1,2,0:T(8,128)(2,1)S(1)} %all-gather), kind=kOutput, calls=%fused_computation.9 | convolution fusion | flops 679624704 | bytes 6193152 | tf_op jit(solution)/shard_map/dot_general | solution.py:8
  193.1 0.9 pad_maximum_fusion.1
  194.0 0.2 reduce-scatter.6.cloned.1.call-start
  194.3 6.7 %convolution_convert_fusion = bf16[512,1152]{1,0:T(8,128)(2,1)S(1)} fusion(bf16[512,2304]{0,1:T(8,128)(2,1)} %all-gather.6.cloned.1.call-done, bf16[2304,1152]{1,0:T(8,128)(2,1)} %param.7), kind=kOutput, calls=%fused_computation | convolution fusion | flops 2718498816 | bytes 8847360 | tf_op jit(solution)/shard_map/dot_general | solution.py:9
  201.0 5.9 %convolution_convert_fusion.1 = bf16[512,1152]{1,0:T(8,128)(2,1)S(1)} fusion(bf16[512,2304]{0,1:T(8,128)(2,1)S(1)} %copy-done.1, bf16[2304,1152]{1,0:T(8,128)(2,1)} %param.6), kind=kOutput, calls=%fused_computation.1 | convolution fusion | flops 2718498816 | bytes 8847360 | tf_op jit(solution)/shard_map/dot_general | solution.py:8
  206.9 1.6 pad_maximum_fusion
  208.5 0.9 convert_element_type.43
  209.4 0.9 convert_element_type.41
  210.4 0.9 convert_element_type.39
  211.3 54.7 %reduce-scatter.8.cloned.1.call-done = bf16[16,2304]{1,0:T(8,128)(2,1)} async-done(((bf16[128,2304]{1,0:T(8,128)(2,1)}), bf16[16,2304]{1,0:T(8,128)(2,1)}) %reduce-scatter.8.cloned.1.call-update) | async-done | bytes 73744 | tf_op jit(solution)/shard_map/reduce_scatter | solution.py:35
  266.0 0.9 convert_element_type.37
  267.0 0.7 pad_maximum_fusion.5
  267.7 36.1 %reduce-scatter.6.cloned.1.call-done = bf16[64,2304]{1,0:T(8,128)(2,1)} async-done(((bf16[512,2304]{1,0:T(8,128)(2,1)}), bf16[64,2304]{1,0:T(8,128)(2,1)}) %reduce-scatter.6.cloned.1.call-update) | async-done | bytes 294928 | tf_op jit(solution)/shard_map/reduce_scatter | solution.py:26
  303.8 1.0 convert_element_type.35
  304.8 0.8 fusion.8
  (21 shorter events, 0.5 us)
Async XLA Ops:
  8.0 186.3 %all-gather.6.cloned.1.call-start = ((), (), s32[]{:S(2)}) async-start(), calls=%async_computation.5 | async-start | bytes 2433024 | tf_op jit(solution)/shard_map/all_gather | solution.py:25
  8.7 199.8 %reduce-scatter.14.cloned.1.call-start = ((), (), s32[]{:S(2)}) async-start(), calls=%async_computation.10 | async-start | bytes 663552 | tf_op jit(solution)/shard_map/reduce_scatter | solution.py:35
  8.8 48.2 %copy-start = (bf16[2304,1152]{1,0:T(8,128)(2,1)S(1)}, bf16[2304,1152]{1,0:T(8,128)(2,1)}, u32[]{:S(2)}) copy-start(bf16[2304,1152]{1,0:T(8,128)(2,1)} %param.6) | copy-start | bytes 15925252
  58.9 150.6 %reduce-scatter.12.cloned.1.call-start = ((), (), s32[]{:S(2)}) async-start(), calls=%async_computation.9 | async-start | bytes 663552 | tf_op jit(solution)/shard_map/reduce_scatter | solution.py:35
  106.0 104.4 %reduce-scatter.10.cloned.1.call-start = ((), (), s32[]{:S(2)}) async-start(), calls=%async_computation.8 | async-start | bytes 663552 | tf_op jit(solution)/shard_map/reduce_scatter | solution.py:35
  150.2 115.8 %reduce-scatter.8.cloned.1.call-start = ((), (), s32[]{:S(2)}) async-start(), calls=%async_computation.7 | async-start | bytes 663552 | tf_op jit(solution)/shard_map/reduce_scatter | solution.py:35
  194.0 109.8 %reduce-scatter.6.cloned.1.call-start = ((), (), s32[]{:S(2)}) async-start(), calls=%async_computation.6 | async-start | bytes 2654208 | tf_op jit(solution)/shard_map/reduce_scatter | solution.py:26
  194.3 6.7 %copy-start.1 = (bf16[512,2304]{0,1:T(8,128)(2,1)S(1)}, bf16[512,2304]{0,1:T(8,128)(2,1)}, u32[]{:S(2)}) copy-start(bf16[512,2304]{0,1:T(8,128)(2,1)} %all-gather.6.cloned.1.call-done) | copy-start | bytes 7077892
Sparse Core Ops, SparseCore 0:
  11.4 79.0 all-gather.5
Sparse Core Ops, SparseCore 1:
  59.0 40.0 reduce-scatter.13
  106.0 48.2 reduce-scatter.11
  156.7 53.5 reduce-scatter.9
  212.8 53.1 reduce-scatter.7
  268.6 35.2 reduce-scatter.5
where the time goes:
time: 315 us; the launch traced here: 313 us
  blocking collectives  155 us (49%)
  waiting for transfers between devices  91.7 us (29%)
  matrix products  38 us (12%)
  between operations  15.9 us (5%)
  other arithmetic  11.2 us (4%)
    all_gather x4, blocking collectives, shards(): lax.all_gather(decode_tokens[step_index], 'gy', axis=1, tiled=True)  155 us
    reduce_scatter x4, waiting for transfers between devices, shards(): lax.psum_scatter(make_terms(current, gate_weight, up_weight).astype(jnp.b...  54.8 us
    reduce_scatter x1, waiting for transfers between devices, shards(): lax.psum_scatter(make_terms(gathered, gate_weight, up_weight).astype(jnp....  36.1 us
    dot_general x5, matrix products, both_terms(): up_part = jnp.dot(rows_in, up_weight, preferred_element_type=jnp.float32)  20.6 us
    dot_general x5, matrix products, both_terms(): jnp.dot(rows_in, gate_weight, preferred_element_type=jnp.float32)  17.3 us
  transfers between devices with their start and end apart: 6, of which 2 were waited for; matrix products, arithmetic and copies ran while one was open for 15% of the time, Pallas kernels for 0%

commit v1 on v0

v1 whole, which is shorter than its diff:
```python
import functools

import jax
import jax.numpy as jnp
from jax import lax
from jax.experimental import pallas as pl
from jax.experimental.pallas import tpu as pltpu
from jax.sharding import PartitionSpec as P

MESH = pl.DeviceIdType.MESH
NX, NZ, NY = 4, 8, 4
CHUNKS = 4
THIRDS = 3
GROUPS = CHUNKS * THIRDS
BF16, F32 = jnp.bfloat16, jnp.float32


def kernel(prompt, decode, gate, up, out_p, out_d, pieces, wbuf, xs, tails, own, psend, precv,
           s1_out, s1_in, s2_out, s2_in, ag_send, ag_recv, rs_send, rs_recv, w_sem):
    gx, gy = lax.axis_index("gx"), lax.axis_index("gy")
    x, core = gx // 2, gx % 2
    z, y = gy // NY, gy % NY

    def at_x(shift):
        return lax.rem(x + shift + NX, NX)

    def at_y(shift):
        return lax.rem(y + shift + NY, NY)

    def at_z(shift):
        return lax.rem(z + shift + NZ, NZ)

    other_core = {"gx": x * 2 + (1 - core), "gy": gy}
    x_up, x_down = ({"gx": at_x(s) * 2 + core, "gy": gy} for s in (1, -1))
    y_up, y_down = ({"gx": gx, "gy": z * NY + at_y(s)} for s in (1, -1))
    z_up, z_down = ({"gx": gx, "gy": at_z(s) * NY + y} for s in (1, -1))

    for j in range(9):
        for half, source in enumerate((gate, up)):
            for begin, rows, to in ((0, 64, 0), (80, 64, 64), (64, 16, 128)):
                pltpu.make_async_copy(
                    source.at[:, pl.ds(begin, rows), pl.ds(128 * j, 128)],
                    wbuf.at[j, :, pl.ds(to, rows), pl.ds(128 * half, 128)],
                    w_sem.at[j],
                ).start()

    barrier = pltpu.get_barrier_semaphore()
    for device in (other_core, x_up, x_down, y_up, y_down, z_up, z_down):
        pl.semaphore_signal(barrier, inc=1, device_id=device, device_id_type=MESH)

    odd = y % 2

    def picks(shape, row_of, col_of):
        r = lax.broadcasted_iota(jnp.int32, shape, 0)
        c = lax.broadcasted_iota(jnp.int32, shape, 1)
        return jnp.where(row_of(r, c) & col_of(r, c), 1.0, 0.0).astype(BF16)

    def main_pick(to_high):
        return picks((72, 128), lambda r, c: (r - 8 * odd) == (c - 64 * to_high),
                     lambda r, c: (c - 64 * to_high >= 0) & (c - 64 * to_high < 64))

    def tail_pick(to_high):
        return picks((16, 72), lambda r, c: c == (r - 8 * to_high) + 64 * (1 - odd),
                     lambda r, c: (r - 8 * to_high >= 0) & (r - 8 * to_high < 8))

    main_top, main_bottom = main_pick(odd), main_pick(1 - odd)
    tail_top, tail_bottom = tail_pick(odd), tail_pick(1 - odd)

    def chunk_rows(c, half):
        if c < 2:
            parts = [prompt[pl.ds(64 * (2 * q + half) + 32 * c, 32), :] for q in range(NX)]
        else:
            parts = [decode[2 * (c - 2) + s, pl.ds(16 * (2 * q + half), 16), :]
                     for q in range(NX) for s in range(2)]
        return jnp.concatenate(parts, axis=0)

    def pack(c):
        top, bottom = chunk_rows(c, 0), chunk_rows(c, 1)
        main = jnp.dot(top, main_top, preferred_element_type=F32)
        main += jnp.dot(bottom, main_bottom, preferred_element_type=F32)
        nt = (((1,), (1,)), ((), ()))
        tail = lax.dot_general(tail_top, top, nt, preferred_element_type=F32)
        tail += lax.dot_general(tail_bottom, bottom, nt, preferred_element_type=F32)
        pieces[c, z, y, 0:128, :] = main.astype(BF16)
        pieces[c, z, y, 128:144, :] = tail.astype(BF16)

    def ag(c, i):
        a_rows, b_rows = pl.ds(0, 64), pl.ds(64, 80)

        def piece(zi, yi, rows):
            return pieces.at[c, zi, yi, rows, :]

        if i in (0, 1):
            view = piece(z, y, a_rows)
        elif i == 2:
            view = piece(z, at_y(-1), pl.ds(0, 32))
        elif i == 3:
            view = piece(z, at_y(1), pl.ds(32, 32))
        elif i < 10:
            s = (i - 4) // 2
            view = piece(at_z(-s if i % 2 == 0 else s), slice(None), a_rows)
        elif i == 10:
            view = piece(at_z(-3), pl.ds(0, 2), a_rows)
        elif i == 11:
            view = piece(at_z(3), pl.ds(2, 2), a_rows)
        elif i < 18:
            s = (i - 12) // 2
            view = piece(at_z(-s if i % 2 == 0 else s), y, b_rows)
        elif i == 18:
            view = piece(at_z(-3), y, pl.ds(64, 48))
        elif i == 19:
            view = piece(at_z(3), y, pl.ds(112, 32))
        elif i in (20, 21):
            view = piece(slice(None), y, b_rows)
        elif i == 22:
            view = piece(pl.ds(0, 4), at_y(-1), b_rows)
        else:
            view = piece(pl.ds(4, 4), at_y(1), b_rows)
        on_y = i < 4 or i >= 20
        device = ((y_up, y_down) if on_y else (z_up, z_down))[i % 2]
        return pltpu.make_async_remote_copy(
            src_ref=view, dst_ref=view, send_sem=ag_send.at[c, i], recv_sem=ag_recv.at[c, i],
            device_id=device, device_id_type=MESH)

    stage_of = [(0, 1, 12, 13), (2, 3, 14, 15), (4, 5, 16, 17), (6, 7, 18, 19), (8, 9, 20, 21), (10, 11, 22, 23)]

    def gather_stage(c, k):
        if k == 0:
            pack(c)
            for i in stage_of[0]:
                ag(c, i).start()
            return
        if k == 6:
            for i in stage_of[5]:
                ag(c, i).wait_recv()
            return
        before, now = stage_of[k - 1], stage_of[k]
        for pair in (0, 2):
            crossing = (k == 2 and pair == 0) or (k == 4 and pair == 2)
            if crossing:
                ag(c, before[pair]).wait_recv()
                ag(c, before[pair + 1]).wait_recv()
                ag(c, now[pair]).start()
                ag(c, now[pair + 1]).start()
            else:
                for way in (0, 1):
                    ag(c, before[pair + way]).wait_recv()
                    ag(c, now[pair + way]).start()

    own_at = pl.multiple_of(core * 128, 128)
    other_at = pl.multiple_of((1 - core) * 128, 128)

    def unpack(c):
        low = lax.broadcasted_iota(jnp.int32, (128, 128), 1) < 64
        first = lax.broadcasted_iota(jnp.int32, (16, 128), 0) < 8

        def body(zi, carry):
            for yp in range(2):
                m = zi * 2 + yp
                e = pieces[c, zi, 2 * yp, 0:128, :].astype(F32)
                o = pieces[c, zi, 2 * yp + 1, 0:128, :].astype(F32)
                lanes = pl.ds(pl.multiple_of(m * 128, 128), 128)
                xs[pl.ds(own_at, 128), lanes] = jnp.where(low, e, o).astype(BF16)
                xs[pl.ds(other_at, 128), lanes] = pltpu.roll(jnp.where(low, o, e), 64, 1).astype(BF16)
                te = pieces[c, zi, 2 * yp, 128:144, :].astype(F32)
                to = pieces[c, zi, 2 * yp + 1, 128:144, :].astype(F32)
                tails[m, :, pl.ds(own_at, 128)] = jnp.where(first, te, to)
                tails[m, :, pl.ds(other_at, 128)] = pltpu.roll(jnp.where(first, to, te), 8, 0)
            return carry

        lax.fori_loop(0, NZ, body, 0)
        xs[:, 2048:2304] = tails[...].reshape(256, 256).T.astype(BF16)

    def rs(g, i):
        if i == 0:
            src, dst, device = psend.at[g], precv.at[g], other_core
        elif i < 3:
            src, dst, device = s1_out.at[g, i - 1], s1_in.at[g, i - 1], (x_down, x_up)[i - 1]
        else:
            src, dst, device = s2_out.at[g, i - 3], s2_in.at[g, i - 3], (x_down, x_up)[i - 3]
        return pltpu.make_async_remote_copy(
            src_ref=src, dst_ref=dst, send_sem=rs_send.at[g, i], recv_sem=rs_recv.at[g, i],
            device_id=device, device_id_type=MESH)

    def multiply(g):
        n = g % THIRDS

        def body(jj, carry):
            j = n * 3 + jj
            w_main = wbuf[j, :, 0:128, :].reshape(2048, 256)
            w_tail = wbuf[j, :, 128:144, :].reshape(256, 256)
            acc = jnp.dot(xs[:, 0:2048], w_main, preferred_element_type=F32)
            acc += jnp.dot(xs[:, 2048:2304], w_tail, preferred_element_type=F32)
            own[g % 4, jj] = acc[0:128]
            psend[g, jj] = acc[128:256].astype(BF16)
            return carry

        lax.fori_loop(0, 3, body, 0)
        rs(g, 0).start()

    def block(shift):
        return pl.ds(pl.multiple_of(at_x(shift) * 32, 32), 32)

    def reduce_1(g):
        rs(g, 0).wait_recv()
        total = own[g % 4] + precv[g].astype(F32)
        own[g % 4] = total
        far = own[g % 4, :, block(2), :].astype(BF16)
        s1_out[g, 0] = far[:, 0:16]
        s1_out[g, 1] = far[:, 16:32]
        rs(g, 1).start()
        rs(g, 2).start()

    def reduce_2(g):
        rs(g, 1).wait_recv()
        down = own[g % 4, :, block(-1), :]
        s2_out[g, 0, :, 0:16] = (down[:, 0:16] + s1_in[g, 0].astype(F32)).astype(BF16)
        s2_out[g, 0, :, 16:32] = down[:, 16:32].astype(BF16)
        rs(g, 3).start()
        rs(g, 2).wait_recv()
        above = own[g % 4, :, block(1), :]
        s2_out[g, 1, :, 0:16] = above[:, 0:16].astype(BF16)
        s2_out[g, 1, :, 16:32] = (above[:, 16:32] + s1_in[g, 1].astype(F32)).astype(BF16)
        rs(g, 4).start()

    def reduce_3(g):
        c, n = g // THIRDS, g % THIRDS
        rs(g, 3).wait_recv()
        rs(g, 4).wait_recv()
        total = own[g % 4, :, block(0), :] + s2_in[g, 0].astype(F32) + s2_in[g, 1].astype(F32)
        for jj in range(3):
            gate_sum, up_sum = total[jj, :, 0:128], total[jj, :, 128:256]
            hidden = (jax.nn.silu(gate_sum) * up_sum).astype(BF16)
            columns = pl.ds(128 * (3 * n + jj), 128)
            if c < 2:
                out_p[pl.ds(32 * c, 32), columns] = hidden
            else:
                out_d[2 * (c - 2), :, columns] = hidden[0:16]
                out_d[2 * (c - 2) + 1, :, columns] = hidden[16:32]

    def turn(g):
        c, n = g // THIRDS, g % THIRDS
        if g < GROUPS:
            if c == 0:
                for j in range(3 * n, 3 * n + 3):
                    pltpu.make_async_copy(wbuf.at[j], wbuf.at[j], w_sem.at[j]).wait()
            if n == 0:
                unpack(c)
            multiply(g)
        for back, step in ((1, reduce_1), (2, reduce_2), (3, reduce_3)):
            if 0 <= g - back < GROUPS:
                step(g - back)

    pl.semaphore_wait(barrier, 7)
    for t in range(13):
        events = [(c, t - 2 * c) for c in range(CHUNKS) if 0 <= t - 2 * c <= 6]
        ready = [3 * ((t - 7) // 2) + 1, 3 * ((t - 7) // 2) + 2] if t >= 7 and t % 2 else []
        for c, k in events:
            gather_stage(c, k)
            if ready:
                turn(ready.pop(0))
        for g in ready:
            turn(g)
        if t >= 6 and t % 2 == 0:
            turn(3 * ((t - 6) // 2))
    turn(10)
    turn(11)
    for g in range(GROUPS, GROUPS + 3):
        turn(g)

    for c in range(CHUNKS):
        for i in range(24):
            ag(c, i).wait_send()
    for g in range(GROUPS):
        for i in range(5):
            rs(g, i).wait_send()


def shards(prompt_tokens, decode_tokens, gate_weight, up_weight):
    gate_weight = gate_weight.reshape(16, 144, 1152)
    up_weight = up_weight.reshape(16, 144, 1152)
    vmem = pl.BlockSpec(memory_space=pltpu.VMEM)
    anywhere = pl.BlockSpec(memory_space=pl.ANY)
    return pl.pallas_call(
        kernel,
        out_shape=(jax.ShapeDtypeStruct((64, 1152), BF16), jax.ShapeDtypeStruct((4, 16, 1152), BF16)),
        in_specs=[vmem, vmem, anywhere, anywhere],
        out_specs=(vmem, vmem),
        scratch_shapes=[
            pltpu.VMEM((CHUNKS, NZ, NY, 144, 128), BF16),
            pltpu.VMEM((9, 16, 144, 256), BF16),
            pltpu.VMEM((256, 2304), BF16),
            pltpu.VMEM((16, 16, 256), F32),
            pltpu.VMEM((4, 3, 128, 256), F32),
            pltpu.VMEM((GROUPS, 3, 128, 256), BF16),
            pltpu.VMEM((GROUPS, 3, 128, 256), BF16),
            pltpu.VMEM((GROUPS, 2, 3, 16, 256), BF16),
            pltpu.VMEM((GROUPS, 2, 3, 16, 256), BF16),
            pltpu.VMEM((GROUPS, 2, 3, 32, 256), BF16),
            pltpu.VMEM((GROUPS, 2, 3, 32, 256), BF16),
            pltpu.SemaphoreType.DMA((CHUNKS, 24)),
            pltpu.SemaphoreType.DMA((CHUNKS, 24)),
            pltpu.SemaphoreType.DMA((GROUPS, 5)),
            pltpu.SemaphoreType.DMA((GROUPS, 5)),
            pltpu.SemaphoreType.DMA((9,)),
        ],
        compiler_params=pltpu.CompilerParams(
            collective_id=0, has_side_effects=True, vmem_limit_bytes=56 * 1024 * 1024),
        cost_estimate=pl.CostEstimate(flops=2 * 1024 * 2304 * 2304, bytes_accessed=11_000_000, transcendentals=147456),
    )(prompt_tokens, decode_tokens, gate_weight, up_weight)


def solution(mesh):
    in_specs = (P(None, ("gx", "gy")), P(None, None, ("gx", "gy")), P("gx", "gy"), P("gx", "gy"))
    out_specs = (P("gx", "gy"), P(None, "gx", "gy"))
    return jax.shard_map(shards, mesh=mesh, in_specs=in_specs, out_specs=out_specs, check_vma=False)
```

time: 315 us -> 97.4 us (0.31)
  blocking collectives: 155 us -> 0 us
  waiting for transfers between devices: 91.7 us -> 0 us
  Pallas kernels: 0 us -> 90.1 us
  matrix products: 38 us -> 0 us
  between operations: 15.9 us -> 0.64 us
  other arithmetic: 11.2 us -> 0 us
  local copies, waits for them, and re-layouts: 0.94 us -> 6.45 us
    all_gather x4 -> x0, blocking collectives: 155 us -> none  [shards(): lax.all_gather(decode_tokens[step_index], 'gy', axis=1, tiled=True)]
    reduce_scatter x5 -> x0, waiting for transfers between devices: 90.9 us -> none  [the longest x4 54.8 us: shards(): lax.psum_scatter(make_terms(current, gate_weight, up_weight).astype(jnp.b...]
    pallas_call x0 -> x1, Pallas kernels: none -> 90.1 us  [shards(): pl.pallas_call(kernel, out_shape=(jax.ShapeDtypeStruct((64, 1152), BF16),...]
    dot_general x10 -> x0, matrix products: 38 us -> none  [the longest x5 20.6 us: both_terms(): up_part = jnp.dot(rows_in, up_weight, preferred_element_type=jnp.float32)]
    unnamed x4, local copies, waits for them, and re-layouts: 0.01 us -> 6.45 us
    convert_element_type x6 -> x0, other arithmetic: 5.34 us -> none  [the longest x4 3.58 us: shards(): summed = lax.psum_scatter(make_terms(current, gate_weight, up_weight).ast...]
    concatenate x5 -> x0, other arithmetic: 5.03 us -> none  [both_terms(): return jnp.concatenate([gate_part, up_part], axis=-1)]
  transfers between devices with their start and end apart: 6 -> 0, of which waited for: 2 -> 0; matrix products, arithmetic and copies ran while one was open for 15% -> 0% of each run, Pallas kernels for 0% -> 0%
where the time goes in v1:
time: 97.4 us; the launch traced here: 97.2 us
  Pallas kernels  90.1 us (93%)
  local copies, waits for them, and re-layouts  6.45 us (7%)
    pallas_call x1, Pallas kernels, shards(): pl.pallas_call(kernel, out_shape=(jax.ShapeDtypeStruct((64, 1152), BF16),...  90.1 us
    unnamed x4, local copies, waits for them, and re-layouts  6.45 us

profile of v1, /device:TPU:1, one launch (start us, length us, event | category | flops | bytes accessed | tf_op | source)
XLA Modules:
  0.0 97.2 jit_solution(5770963919131058866)
XLA Ops:
  0.6 1.6 %copy.6.prompt = bf16[512,72]{1,0:T(8,128)(2,1)} copy(bf16[512,72]{0,1:T(8,128)(2,1)} %param.4) | data formatting | bytes 147456 | tf_op args[0]
  2.3 1.6 %copy.7.decode = bf16[4,128,72]{2,1,0:T(8,128)(2,1)} copy(bf16[4,128,72]{1,2,0:T(8,128)(2,1)} %param.5) | data formatting | bytes 147456 | tf_op args[1]
  3.9 90.1 %shard_map.59 = (bf16[64,1152]{1,0:T(8,128)(2,1)}, bf16[4,16,1152]{2,1,0:T(8,128)(2,1)}) custom-call(bf16[512,72]{1,0:T(8,128)(2,1)} %copy.6.prompt, bf16[4,128,72]{2,1,0:T(8,128)(2,1)} %copy.7.decode, bf16[16,144,1152]{2,1,0:T(8,128)(2,1)} %bitcast.2, bf16[16,144,1152]{2,1,0:T(8,128)(2,1)} %bitcast.3), custom_call_target="tpu_custom_call" | custom-call | flops 10871635968 | bytes 11000000 | tf_op jit(solution)/shard_map/pallas_call | solution.py:284
  94.0 1.6 %copy.10 = bf16[64,1152]{1,0:T(8,128)(2,1)} copy(bf16[64,1152]{1,0:T(8,128)(2,1)} %get-tuple-element.4) | data formatting | bytes 294912
  95.6 1.6 %copy.11 = bf16[4,16,1152]{2,1,0:T(8,128)(2,1)} copy(bf16[4,16,1152]{2,1,0:T(8,128)(2,1)} %get-tuple-element.5) | data formatting | bytes 294912

commit v2 on v0

v2 whole, which is shorter than its diff:
```python
import functools

import jax
import jax.numpy as jnp
from jax import lax
from jax.experimental import pallas as pl
from jax.experimental.pallas import tpu as pltpu
from jax.sharding import PartitionSpec as P

MESH = pl.DeviceIdType.MESH
NX, NZ, NY = 4, 8, 4
CHUNKS, THIRDS = 4, 3
GROUPS = CHUNKS * THIRDS
BF16, F32 = jnp.bfloat16, jnp.float32

SPLIT = (64, 32, 64, 64)
STRAIGHT = (False, False, False, False)
SETS = (((0, 3), (3, 5), (5, 8)), ((0, 3), (3, 8)), ((0, 3), (3, 5), (5, 8)), ((0, 8),))
SHORT = (11,)
ORDER = (
    ("pack", 0, 0), ("pack", 1, 0), ("B1", 0, 0), ("Y", 0, 0), ("B1", 1, 0), ("Y", 1, 0), ("A1", 0, 0), ("A1", 1, 0),
    ("pack", 2, 0), ("pack", 3, 0), ("B2", 0, 0), ("Y", 0, 1), ("B2", 1, 0), ("E", 0, 0), ("A2", 0, 0), ("E", 1, 0),
    ("A2", 1, 0), ("B1", 2, 0), ("Y", 2, 0), ("B1", 3, 0), ("A1", 2, 0), ("A1", 3, 0), ("Y", 0, 2), ("E", 0, 1),
    ("Y", 1, 1), ("A3", 0, 0), ("E", 2, 0), ("A3", 1, 0), ("B2", 2, 0), ("Y", 2, 1), ("B2", 3, 0), ("E", 0, 2),
    ("A2", 2, 0), ("A2", 3, 0), ("E", 1, 1), ("E", 2, 1), ("U", 0, 0), ("MM", 0, 0), ("MM", 1, 0), ("Y", 2, 2),
    ("Y", 3, 0), ("MM", 2, 0), ("R1", 0, 0), ("R1", 1, 0), ("A3", 2, 0), ("U", 1, 0), ("MM", 3, 0), ("R1", 2, 0),
    ("A3", 3, 0), ("MM", 4, 0), ("R2", 0, 0), ("R1", 3, 0), ("R2", 1, 0), ("E", 2, 2), ("MM", 5, 0), ("R1", 4, 0),
    ("R2", 2, 0), ("E", 3, 0), ("R1", 5, 0), ("R3", 0, 0), ("U", 2, 0), ("R2", 3, 0), ("MM", 6, 0), ("R3", 1, 0),
    ("R2", 4, 0), ("MM", 7, 0), ("R1", 6, 0), ("R3", 2, 0), ("R2", 5, 0), ("MM", 8, 0), ("R1", 7, 0), ("R3", 3, 0),
    ("U", 3, 0), ("MM", 9, 0), ("R1", 8, 0), ("R2", 6, 0), ("R3", 4, 0), ("MM", 10, 0), ("R2", 7, 0), ("R1", 9, 0),
    ("R3", 5, 0), ("MM", 11, 0), ("R1", 10, 0), ("R2", 8, 0), ("R3", 6, 0), ("R1", 11, 0), ("R3", 7, 0),
    ("R2", 9, 0), ("R2", 10, 0), ("R3", 8, 0), ("R3", 9, 0), ("R3", 10, 0), ("R3", 11, 0),
)

SLOT = {0: 0, -1: 1, 1: 2, -2: 3, 2: 4, -3: 5, 3: 6, 4: 7, -4: 7}
DISTANCE = (0, 1, 1, 2, 2, 3, 3, 4)


def rows_of(c, which):
    split = SPLIT[c]
    half = {96: 48, 80: 48, 112: 64, 128: 64}[144 - split]
    begin, size = {"a": (0, split), "b": (split, 144 - split), "low": (split, half), "high": (split + half, 144 - split - half)}[which]
    return pl.ds(begin, size)


def plan(c):
    copies = {"a1p": (0, 0, "a", 0, ("y", 1)), "a1m": (0, 0, "a", 0, ("y", -1)), "a1x": (0, 0, "a", 0, ("y", 2))}
    for s, way in ((1, "p"), (-1, "m")):
        for d in (1, 2, 3):
            copies[f"c{d}{way}"] = (SLOT[-s * (d - 1)], None, "a", SLOT[-s * d], ("z", s))
        copies[f"c4{way}"] = (SLOT[-2 * s], "pair" + way, "a", 7, ("z", 2 * s))
        if STRAIGHT[c]:
            for d in (1, 2, 3):
                copies[f"b{d}{way}"] = (0, 0, "b", SLOT[-s * d], ("z", s * d))
        else:
            for d in (1, 2, 3):
                copies[f"b{d}{way}"] = (SLOT[-s * (d - 1)], 0, "b", SLOT[-s * d], ("z", s))
            copies[f"b4{way}"] = (SLOT[-2 * s], 0, "low" if s > 0 else "high", 7, ("z", 2 * s))
        for i, (lo, hi) in enumerate(SETS[c]):
            copies[f"d{i}{way}"] = ((lo, hi), 0, "b", (lo, hi), ("y", s))
            copies[f"e{i}{way}"] = ((lo, hi), -s, "low" if s > 0 else "high", (lo, hi), ("y", s))
    if STRAIGHT[c]:
        copies["b4"] = (0, 0, "b", 7, ("z", 4))
    return copies


PLANS = [plan(c) for c in range(CHUNKS)]
COPY_INDEX = [{name: i for i, name in enumerate(p)} for p in PLANS]
MOST = max(len(p) for p in PLANS)


def steps(c):
    straight = STRAIGHT[c]
    table = {
        ("A1", 0): (("a1p", "a1m", "a1x"), ("c1p", "c1m")),
        ("A2", 0): (("c1p", "c1m"), ("c2p", "c2m")),
        ("A3", 0): (("c2p", "c2m"), ("c4p", "c4m", "c3p", "c3m")),
    }
    first = ["a1p", "a1m", "a1x"]
    if straight:
        first += ["b1p", "b1m", "b2p", "b2m", "b3p", "b3m", "b4"]
    else:
        first += ["b1p", "b1m"]
        table["B1", 0] = (("b1p", "b1m"), ("b2p", "b2m"))
        table["B2", 0] = (("b2p", "b2m"), ("b4p", "b4m", "b3p", "b3m"))
    table["pack", 0] = ((), tuple(first))
    done = ["c3p", "c3m", "c4p", "c4m"]
    for i, (lo, hi) in enumerate(SETS[c]):
        need = []
        for d in sorted(set(DISTANCE[lo:hi])):
            need += {0: [], 4: ["b4"] if straight else ["b4p", "b4m"]}.get(d, [f"b{d}p", f"b{d}m"])
        table["Y", i] = (tuple(need), (f"d{i}p", f"d{i}m"))
        table["E", i] = ((f"d{i}p", f"d{i}m"), (f"e{i}p", f"e{i}m"))
        done += [f"e{i}p", f"e{i}m"]
    table["U", 0] = (tuple(done), ())
    return table


STEPS = [steps(c) for c in range(CHUNKS)]


def kernel(prompt, decode, gate, up, out_p, out_d, pieces, wbuf, xs, tails, own, psend, precv,
           s1_out, s1_in, s2_out, s2_in, ag_send, ag_recv, rs_send, rs_recv, w_sem):
    gx, gy = lax.axis_index("gx"), lax.axis_index("gy")
    x, core = gx // 2, gx % 2
    z, y = gy // NY, gy % NY

    def at_y(shift):
        return lax.rem(y + (shift + NY), NY)

    def at_x(shift):
        return lax.rem(x + (shift + NX), NX)

    def device(axis, shift):
        if axis == "core":
            return {"gx": x * 2 + (1 - core), "gy": gy}
        if axis == "x":
            return {"gx": at_x(shift) * 2 + core, "gy": gy}
        if axis == "y":
            return {"gx": gx, "gy": z * NY + at_y(shift)}
        return {"gx": gx, "gy": lax.rem(z + (shift + NZ), NZ) * NY + y}

    barrier = pltpu.get_barrier_semaphore()
    hops = {("core", 1), ("x", 1), ("x", -1)} | {p[name][4] for p in PLANS for name in p}
    if SHORT:
        hops.add(("x", 2))
    for axis, shift in sorted(hops):
        pl.semaphore_signal(barrier, inc=1, device_id=device(axis, shift), device_id_type=MESH)

    for n in range(THIRDS):
        for half, source in enumerate((gate, up)):
            for begin, rows, to in ((0, 64, 0), (80, 64, 64), (64, 16, 128)):
                pltpu.make_async_copy(
                    source.at[:, pl.ds(begin, rows), pl.ds(384 * n, 384)],
                    wbuf.at[n, :, pl.ds(to, rows), pl.ds(384 * half, 384)],
                    w_sem.at[n],
                ).start()

    odd = y % 2
    nt = (((1,), (1,)), ((), ()))

    def picks(shape, row_of, col_of):
        r = lax.broadcasted_iota(jnp.int32, shape, 0)
        c = lax.broadcasted_iota(jnp.int32, shape, 1)
        return jnp.where(row_of(r, c) & col_of(r, c), 1.0, 0.0).astype(BF16)

    def main_pick(to_high):
        return picks((72, 128), lambda r, c: (r - 8 * odd) == (c - 64 * to_high),
                     lambda r, c: (c - 64 * to_high >= 0) & (c - 64 * to_high < 64))

    def tail_pick(to_high):
        return picks((16, 72), lambda r, c: c == (r - 8 * to_high) + 64 * (1 - odd),
                     lambda r, c: (r - 8 * to_high >= 0) & (r - 8 * to_high < 8))

    main_top, main_bottom = main_pick(odd), main_pick(1 - odd)
    tail_top, tail_bottom = tail_pick(odd), tail_pick(1 - odd)

    def chunk_rows(c, half):
        def row_pick(columns, source_of):
            r = lax.broadcasted_iota(jnp.int32, (128, columns), 0)
            s = lax.broadcasted_iota(jnp.int32, (128, columns), 1)
            return jnp.where(source_of(r) == s, 1.0, 0.0).astype(BF16)

        if c < 2:
            pick = row_pick(512, lambda r: (r // 32) * 128 + 64 * half + 32 * c + r % 32)
            got = lax.dot_general(pick, prompt[...], nt, preferred_element_type=F32)
        else:
            got = 0.0
            for s in range(2):
                pick = row_pick(128, lambda r: jnp.where((r % 32) // 16 == s, (r // 32) * 32 + 16 * half + r % 16, -1))
                got += lax.dot_general(pick, decode[2 * (c - 2) + s], nt, preferred_element_type=F32)
        return got.astype(BF16)

    def pack(c):
        top, bottom = chunk_rows(c, 0), chunk_rows(c, 1)
        main = jnp.dot(top, main_top, preferred_element_type=F32)
        main += jnp.dot(bottom, main_bottom, preferred_element_type=F32)
        tail = lax.dot_general(tail_top, top, nt, preferred_element_type=F32)
        tail += lax.dot_general(tail_bottom, bottom, nt, preferred_element_type=F32)
        pieces[c, 0, y, 0:128, :] = main.astype(BF16)
        pieces[c, 0, y, 128:144, :] = tail.astype(BF16)

    def copy(c, name):
        slots, y_shift, rows, to_slots, hop = PLANS[c][name]
        rows = rows_of(c, rows)
        if y_shift is None:
            y_at = slice(None)
        elif y_shift in ("pairp", "pairm"):
            y_at = pl.ds(0 if y_shift == "pairp" else 2, 2)
        else:
            y_at = at_y(y_shift)

        def view(s):
            s = pl.ds(s[0], s[1] - s[0]) if isinstance(s, tuple) else s
            return pieces.at[c, s, y_at, rows, :]

        i = COPY_INDEX[c][name]
        return pltpu.make_async_remote_copy(
            src_ref=view(slots), dst_ref=view(to_slots), send_sem=ag_send.at[c, i], recv_sem=ag_recv.at[c, i],
            device_id=device(*hop), device_id_type=MESH)

    top_at = pl.multiple_of(core * 128, 128)
    bottom_at = pl.multiple_of((1 - core) * 128, 128)

    def unpack(c):
        low = lax.broadcasted_iota(jnp.int32, (128, 128), 1) < 64
        first = lax.broadcasted_iota(jnp.int32, (16, 128), 0) < 8

        def body(slot, carry):
            away = (slot + 1) // 2
            source = lax.rem(z + jnp.where(slot % 2 == 0, away, NZ - away), NZ)
            for yp in range(2):
                m = source * 2 + yp
                e = pieces[c, slot, 2 * yp, 0:128, :].astype(F32)
                o = pieces[c, slot, 2 * yp + 1, 0:128, :].astype(F32)
                lanes = pl.ds(pl.multiple_of(m * 128, 128), 128)
                xs[pl.ds(top_at, 128), lanes] = jnp.where(low, e, o).astype(BF16)
                xs[pl.ds(bottom_at, 128), lanes] = pltpu.roll(jnp.where(low, o, e), 64, 1).astype(BF16)
                te = pieces[c, slot, 2 * yp, 128:144, :].astype(F32)
                to = pieces[c, slot, 2 * yp + 1, 128:144, :].astype(F32)
                tails[m, :, pl.ds(top_at, 128)] = jnp.where(first, te, to)
                tails[m, :, pl.ds(bottom_at, 128)] = pltpu.roll(jnp.where(first, to, te), 8, 0)
            return carry

        lax.fori_loop(0, NZ, body, 0)
        xs[:, 2048:2304] = tails[...].reshape(256, 256).T.astype(BF16)

    def rs(g, name):
        i = ("pair", "far_down", "far_up", "down", "up", "across").index(name)
        if i == 0:
            src, dst, to = psend.at[g], precv.at[g], ("core", 1)
        elif i < 3:
            src, dst, to = s1_out.at[g, i - 1], s1_in.at[g, i - 1], ("x", (-1, 1)[i - 1])
        else:
            src, dst, to = s2_out.at[g, i - 3], s2_in.at[g, i - 3], ("x", (-1, 1, 2)[i - 3])
        return pltpu.make_async_remote_copy(
            src_ref=src, dst_ref=dst, send_sem=rs_send.at[g, i], recv_sem=rs_recv.at[g, i],
            device_id=device(*to), device_id_type=MESH)

    def multiply(g):
        n = g % THIRDS
        if g < THIRDS:
            pltpu.make_async_copy(wbuf.at[n], wbuf.at[n], w_sem.at[n]).wait()
        acc = jnp.dot(xs[:, 0:2048], wbuf[n, :, 0:128, :].reshape(2048, 768), preferred_element_type=F32)
        acc += jnp.dot(xs[:, 2048:2304], wbuf[n, :, 128:144, :].reshape(256, 768), preferred_element_type=F32)
        psend[g] = acc[128:256].astype(BF16)
        rs(g, "pair").start()
        own[g % 6] = acc[0:128]

    def block(shift):
        return pl.ds(pl.multiple_of(at_x(shift) * 32, 32), 32)

    def reduce_1(g):
        rs(g, "pair").wait_recv()

        def pair_sum(shift):
            rows = block(shift)
            return own[g % 6, rows, :] + precv[g, rows, :].astype(F32)

        if g in SHORT:
            for i, (name, shift) in enumerate((("down", -1), ("up", 1), ("across", 2))):
                s2_out[g, i] = pair_sum(shift).astype(BF16)
            for name in ("across", "down", "up"):
                rs(g, name).start()
        else:
            far = pair_sum(2).astype(BF16)
            s1_out[g, 0] = far[0:16]
            s1_out[g, 1] = far[16:32]
            rs(g, "far_down").start()
            rs(g, "far_up").start()
            for shift in (-1, 1):
                own[g % 6, block(shift), :] = pair_sum(shift)
        own[g % 6, block(0), :] = pair_sum(0)

    def reduce_2(g):
        rs(g, "far_down").wait_recv()
        rs(g, "far_up").wait_recv()
        below, above = own[g % 6, block(-1), :], own[g % 6, block(1), :]
        s2_out[g, 0, 0:16] = (below[0:16] + s1_in[g, 0].astype(F32)).astype(BF16)
        s2_out[g, 0, 16:32] = below[16:32].astype(BF16)
        rs(g, "down").start()
        s2_out[g, 1, 0:16] = above[0:16].astype(BF16)
        s2_out[g, 1, 16:32] = (above[16:32] + s1_in[g, 1].astype(F32)).astype(BF16)
        rs(g, "up").start()

    def reduce_3(g):
        c, n = g // THIRDS, g % THIRDS
        rs(g, "down").wait_recv()
        rs(g, "up").wait_recv()
        total = own[g % 6, block(0), :] + s2_in[g, 0].astype(F32) + s2_in[g, 1].astype(F32)
        if g in SHORT:
            rs(g, "across").wait_recv()
            total += s2_in[g, 2].astype(F32)
        hidden = (jax.nn.silu(total[:, 0:384]) * total[:, 384:768]).astype(BF16)
        columns = pl.ds(384 * n, 384)
        if c < 2:
            out_p[pl.ds(32 * c, 32), columns] = hidden
        else:
            out_d[2 * (c - 2), :, columns] = hidden[0:16]
            out_d[2 * (c - 2) + 1, :, columns] = hidden[16:32]

    greeted, arrived = False, set()
    for kind, number, index in ORDER:
        if kind in ("MM", "R1", "R2", "R3"):
            {"MM": multiply, "R1": reduce_1, "R2": reduce_2, "R3": reduce_3}[kind](number)
            continue
        before, after = STEPS[number][kind, index]
        if kind == "pack":
            pack(number)
            if not greeted:
                pl.semaphore_wait(barrier, len(hops))
                greeted = True
        for name in before:
            if (number, name) not in arrived:
                copy(number, name).wait_recv()
                arrived.add((number, name))
        for name in after:
            copy(number, name).start()
        if kind == "U":
            unpack(number)

    for c in range(CHUNKS):
        for name in PLANS[c]:
            assert (c, name) in arrived
            copy(c, name).wait_send()
    for g in range(GROUPS):
        for name in ("pair", "down", "up") + (("across",) if g in SHORT else ("far_down", "far_up")):
            rs(g, name).wait_send()


def shards(prompt_tokens, decode_tokens, gate_weight, up_weight):
    gate_weight = gate_weight.reshape(16, 144, 1152)
    up_weight = up_weight.reshape(16, 144, 1152)
    vmem = pl.BlockSpec(memory_space=pltpu.VMEM)
    anywhere = pl.BlockSpec(memory_space=pl.ANY)
    return pl.pallas_call(
        kernel,
        out_shape=(jax.ShapeDtypeStruct((64, 1152), BF16), jax.ShapeDtypeStruct((4, 16, 1152), BF16)),
        in_specs=[vmem, vmem, anywhere, anywhere],
        out_specs=(vmem, vmem),
        scratch_shapes=[
            pltpu.VMEM((CHUNKS, NZ, NY, 144, 128), BF16),
            pltpu.VMEM((THIRDS, 16, 144, 768), BF16),
            pltpu.VMEM((256, 2304), BF16),
            pltpu.VMEM((16, 16, 256), F32),
            pltpu.VMEM((6, 128, 768), F32),
            pltpu.VMEM((GROUPS, 128, 768), BF16),
            pltpu.VMEM((GROUPS, 128, 768), BF16),
            pltpu.VMEM((GROUPS, 2, 16, 768), BF16),
            pltpu.VMEM((GROUPS, 2, 16, 768), BF16),
            pltpu.VMEM((GROUPS, 3, 32, 768), BF16),
            pltpu.VMEM((GROUPS, 3, 32, 768), BF16),
            pltpu.SemaphoreType.DMA((CHUNKS, MOST)),
            pltpu.SemaphoreType.DMA((CHUNKS, MOST)),
            pltpu.SemaphoreType.DMA((GROUPS, 6)),
            pltpu.SemaphoreType.DMA((GROUPS, 6)),
            pltpu.SemaphoreType.DMA((THIRDS,)),
        ],
        compiler_params=pltpu.CompilerParams(
            collective_id=0, has_side_effects=True, vmem_limit_bytes=56 * 1024 * 1024),
        cost_estimate=pl.CostEstimate(flops=2 * 1024 * 2304 * 2304, bytes_accessed=11_000_000, transcendentals=147456),
    )(prompt_tokens.T, decode_tokens.transpose(0, 2, 1), gate_weight, up_weight)


def solution(mesh):
    in_specs = (P(None, ("gx", "gy")), P(None, None, ("gx", "gy")), P("gx", "gy"), P("gx", "gy"))
    out_specs = (P("gx", "gy"), P(None, "gx", "gy"))
    return jax.shard_map(shards, mesh=mesh, in_specs=in_specs, out_specs=out_specs, check_vma=False)
```

time: 315 us -> 79.5 us (0.25)
  blocking collectives: 155 us -> 0 us
  waiting for transfers between devices: 91.7 us -> 0 us
  Pallas kernels: 0 us -> 75.6 us
  matrix products: 38 us -> 0 us
  between operations: 15.9 us -> 0.64 us
  other arithmetic: 11.2 us -> 0 us
    all_gather x4 -> x0, blocking collectives: 155 us -> none  [shards(): lax.all_gather(decode_tokens[step_index], 'gy', axis=1, tiled=True)]
    reduce_scatter x5 -> x0, waiting for transfers between devices: 90.9 us -> none  [the longest x4 54.8 us: shards(): lax.psum_scatter(make_terms(current, gate_weight, up_weight).astype(jnp.b...]
    pallas_call x0 -> x1, Pallas kernels: none -> 75.6 us  [shards(): pl.pallas_call(kernel, out_shape=(jax.ShapeDtypeStruct((64, 1152), BF16),...]
    dot_general x10 -> x0, matrix products: 38 us -> none  [the longest x5 20.6 us: both_terms(): up_part = jnp.dot(rows_in, up_weight, preferred_element_type=jnp.float32)]
    convert_element_type x6 -> x0, other arithmetic: 5.34 us -> none  [the longest x4 3.58 us: shards(): summed = lax.psum_scatter(make_terms(current, gate_weight, up_weight).ast...]
    concatenate x5 -> x0, other arithmetic: 5.03 us -> none  [both_terms(): return jnp.concatenate([gate_part, up_part], axis=-1)]
    unnamed x4 -> x2, local copies, waits for them, and re-layouts: 0.01 us -> 3.16 us
  transfers between devices with their start and end apart: 6 -> 0, of which waited for: 2 -> 0; matrix products, arithmetic and copies ran while one was open for 15% -> 0% of each run, Pallas kernels for 0% -> 0%
where the time goes in v2:
time: 79.5 us; the launch traced here: 79.4 us
  Pallas kernels  75.6 us (95%)
  local copies, waits for them, and re-layouts  3.16 us (4%)
    pallas_call x1, Pallas kernels, shards(): pl.pallas_call(kernel, out_shape=(jax.ShapeDtypeStruct((64, 1152), BF16),...  75.6 us
    unnamed x2, local copies, waits for them, and re-layouts  3.16 us

profile of v2, /device:TPU:1, one launch (start us, length us, event | category | flops | bytes accessed | tf_op | source)
XLA Modules:
  0.0 79.4 jit_solution(328917750755461216)
XLA Ops:
  0.6 75.6 %shard_map.59 = (bf16[64,1152]{1,0:T(8,128)(2,1)}, bf16[4,16,1152]{2,1,0:T(8,128)(2,1)}) custom-call(bf16[72,512]{1,0:T(8,128)(2,1)} %bitcast.6, bf16[4,72,128]{2,1,0:T(8,128)(2,1)} %bitcast.7, bf16[16,144,1152]{2,1,0:T(8,128)(2,1)} %bitcast.4, bf16[16,144,1152]{2,1,0:T(8,128)(2,1)} %bitcast.5), custom_call_target="tpu_custom_call" | custom-call | flops 10871635968 | bytes 11000000 | tf_op jit(solution)/shard_map/pallas_call | solution.py:336
  76.2 1.6 %copy.8 = bf16[64,1152]{1,0:T(8,128)(2,1)} copy(bf16[64,1152]{1,0:T(8,128)(2,1)} %get-tuple-element.4) | data formatting | bytes 294912
  77.8 1.6 %copy.9 = bf16[4,16,1152]{2,1,0:T(8,128)(2,1)} copy(bf16[4,16,1152]{2,1,0:T(8,128)(2,1)} %get-tuple-element.5) | data formatting | bytes 294912

commit v3 on v2

--- a/solution.py
+++ b/solution.py
@@ -13,23 +13,25 @@
 GROUPS = CHUNKS * THIRDS
 BF16, F32 = jnp.bfloat16, jnp.float32
 
-SPLIT = (64, 32, 64, 64)
-STRAIGHT = (False, False, False, False)
-SETS = (((0, 3), (3, 5), (5, 8)), ((0, 3), (3, 8)), ((0, 3), (3, 5), (5, 8)), ((0, 8),))
-SHORT = (11,)
+SPLIT = (32, 64, 48, 48)
+STRAIGHT = (True, True, False, False)
+SETS = (((0, 5), (5, 8)), ((0, 5), (5, 8)), ((0, 5), (5, 8)), ((0, 3), (3, 5), (5, 8)))
+WIDE = (False, False, False, False)
+LEAP = (False, False, False, False)
+SHORT = (8, 9, 10, 11)
 ORDER = (
-    ("pack", 0, 0), ("pack", 1, 0), ("B1", 0, 0), ("Y", 0, 0), ("B1", 1, 0), ("Y", 1, 0), ("A1", 0, 0), ("A1", 1, 0),
-    ("pack", 2, 0), ("pack", 3, 0), ("B2", 0, 0), ("Y", 0, 1), ("B2", 1, 0), ("E", 0, 0), ("A2", 0, 0), ("E", 1, 0),
-    ("A2", 1, 0), ("B1", 2, 0), ("Y", 2, 0), ("B1", 3, 0), ("A1", 2, 0), ("A1", 3, 0), ("Y", 0, 2), ("E", 0, 1),
-    ("Y", 1, 1), ("A3", 0, 0), ("E", 2, 0), ("A3", 1, 0), ("B2", 2, 0), ("Y", 2, 1), ("B2", 3, 0), ("E", 0, 2),
-    ("A2", 2, 0), ("A2", 3, 0), ("E", 1, 1), ("E", 2, 1), ("U", 0, 0), ("MM", 0, 0), ("MM", 1, 0), ("Y", 2, 2),
-    ("Y", 3, 0), ("MM", 2, 0), ("R1", 0, 0), ("R1", 1, 0), ("A3", 2, 0), ("U", 1, 0), ("MM", 3, 0), ("R1", 2, 0),
-    ("A3", 3, 0), ("MM", 4, 0), ("R2", 0, 0), ("R1", 3, 0), ("R2", 1, 0), ("E", 2, 2), ("MM", 5, 0), ("R1", 4, 0),
-    ("R2", 2, 0), ("E", 3, 0), ("R1", 5, 0), ("R3", 0, 0), ("U", 2, 0), ("R2", 3, 0), ("MM", 6, 0), ("R3", 1, 0),
-    ("R2", 4, 0), ("MM", 7, 0), ("R1", 6, 0), ("R3", 2, 0), ("R2", 5, 0), ("MM", 8, 0), ("R1", 7, 0), ("R3", 3, 0),
-    ("U", 3, 0), ("MM", 9, 0), ("R1", 8, 0), ("R2", 6, 0), ("R3", 4, 0), ("MM", 10, 0), ("R2", 7, 0), ("R1", 9, 0),
-    ("R3", 5, 0), ("MM", 11, 0), ("R1", 10, 0), ("R2", 8, 0), ("R3", 6, 0), ("R1", 11, 0), ("R3", 7, 0),
-    ("R2", 9, 0), ("R2", 10, 0), ("R3", 8, 0), ("R3", 9, 0), ("R3", 10, 0), ("R3", 11, 0),
+    ("pack", 0, 0), ("A1", 0, 0), ("pack", 1, 0), ("pack", 2, 0), ("Y", 0, 0), ("A2", 0, 0), ("Y", 0, 1),
+    ("A1", 1, 0), ("Y", 1, 0), ("A1", 2, 0), ("pack", 3, 0), ("E", 0, 0), ("B1", 2, 0), ("A3", 0, 0), ("E", 0, 1),
+    ("A2", 1, 0), ("Y", 1, 1), ("A2", 2, 0), ("B2", 2, 0), ("E", 1, 0), ("A1", 3, 0), ("Y", 2, 0), ("B1", 3, 0),
+    ("U", 0, 0), ("A3", 1, 0), ("MM", 0, 0), ("E", 1, 1), ("MM", 1, 0), ("Y", 2, 1), ("A3", 2, 0), ("R1", 0, 0),
+    ("MM", 2, 0), ("R1", 1, 0), ("E", 2, 0), ("A2", 3, 0), ("B2", 3, 0), ("Y", 3, 0), ("R1", 2, 0), ("U", 1, 0),
+    ("R2", 0, 0), ("Y", 3, 1), ("MM", 3, 0), ("R2", 1, 0), ("E", 2, 1), ("MM", 4, 0), ("R2", 2, 0), ("R1", 3, 0),
+    ("A3", 3, 0), ("Y", 3, 2), ("MM", 5, 0), ("R1", 4, 0), ("E", 3, 0), ("R3", 0, 0), ("U", 2, 0), ("E", 3, 1),
+    ("R1", 5, 0), ("R3", 1, 0), ("MM", 6, 0), ("R2", 3, 0), ("R3", 2, 0), ("E", 3, 2), ("MM", 7, 0), ("R2", 4, 0),
+    ("R1", 6, 0), ("MM", 8, 0), ("R2", 5, 0), ("R1", 7, 0), ("U", 3, 0), ("R1", 8, 0), ("R3", 3, 0), ("MM", 9, 0),
+    ("R2", 6, 0), ("R3", 4, 0), ("MM", 10, 0), ("R2", 7, 0), ("R1", 9, 0), ("R3", 5, 0), ("MM", 11, 0),
+    ("R1", 10, 0), ("R3", 6, 0), ("R1", 11, 0), ("R3", 7, 0), ("R3", 8, 0), ("R3", 9, 0), ("R3", 10, 0),
+    ("R3", 11, 0),
 )
 
 SLOT = {0: 0, -1: 1, 1: 2, -2: 3, 2: 4, -3: 5, 3: 6, 4: 7, -4: 7}
@@ -47,7 +49,8 @@
     copies = {"a1p": (0, 0, "a", 0, ("y", 1)), "a1m": (0, 0, "a", 0, ("y", -1)), "a1x": (0, 0, "a", 0, ("y", 2))}
     for s, way in ((1, "p"), (-1, "m")):
         for d in (1, 2, 3):
-            copies[f"c{d}{way}"] = (SLOT[-s * (d - 1)], None, "a", SLOT[-s * d], ("z", s))
+            leap = 2 if d == 2 and LEAP[c] else 1
+            copies[f"c{d}{way}"] = (SLOT[-s * (d - leap)], None, "a", SLOT[-s * d], ("z", s * leap))
         copies[f"c4{way}"] = (SLOT[-2 * s], "pair" + way, "a", 7, ("z", 2 * s))
         if STRAIGHT[c]:
             for d in (1, 2, 3):
@@ -58,7 +61,10 @@
             copies[f"b4{way}"] = (SLOT[-2 * s], 0, "low" if s > 0 else "high", 7, ("z", 2 * s))
         for i, (lo, hi) in enumerate(SETS[c]):
             copies[f"d{i}{way}"] = ((lo, hi), 0, "b", (lo, hi), ("y", s))
-            copies[f"e{i}{way}"] = ((lo, hi), -s, "low" if s > 0 else "high", (lo, hi), ("y", s))
+            if WIDE[c]:
+                copies[f"x{i}"] = ((lo, hi), 0, "b", (lo, hi), ("y", 2))
+            else:
+                copies[f"e{i}{way}"] = ((lo, hi), -s, "low" if s > 0 else "high", (lo, hi), ("y", s))
     if STRAIGHT[c]:
         copies["b4"] = (0, 0, "b", 7, ("z", 4))
     return copies
@@ -76,6 +82,9 @@
         ("A2", 0): (("c1p", "c1m"), ("c2p", "c2m")),
         ("A3", 0): (("c2p", "c2m"), ("c4p", "c4m", "c3p", "c3m")),
     }
+    if LEAP[c]:
+        table["A1", 0] = (("a1p", "a1m", "a1x"), ("c2p", "c2m", "c1p", "c1m"))
+        del table["A2", 0]
     first = ["a1p", "a1m", "a1x"]
     if straight:
         first += ["b1p", "b1m", "b2p", "b2m", "b3p", "b3m", "b4"]
@@ -84,14 +93,18 @@
         table["B1", 0] = (("b1p", "b1m"), ("b2p", "b2m"))
         table["B2", 0] = (("b2p", "b2m"), ("b4p", "b4m", "b3p", "b3m"))
     table["pack", 0] = ((), tuple(first))
-    done = ["c3p", "c3m", "c4p", "c4m"]
+    done = ["c1p", "c1m", "c3p", "c3m", "c4p", "c4m"]
     for i, (lo, hi) in enumerate(SETS[c]):
         need = []
         for d in sorted(set(DISTANCE[lo:hi])):
             need += {0: [], 4: ["b4"] if straight else ["b4p", "b4m"]}.get(d, [f"b{d}p", f"b{d}m"])
-        table["Y", i] = (tuple(need), (f"d{i}p", f"d{i}m"))
-        table["E", i] = ((f"d{i}p", f"d{i}m"), (f"e{i}p", f"e{i}m"))
-        done += [f"e{i}p", f"e{i}m"]
+        if WIDE[c]:
+            table["Y", i] = (tuple(need), (f"x{i}", f"d{i}p", f"d{i}m"))
+            done += [f"d{i}p", f"d{i}m", f"x{i}"]
+        else:
+            table["Y", i] = (tuple(need), (f"d{i}p", f"d{i}m"))
+            table["E", i] = ((f"d{i}p", f"d{i}m"), (f"e{i}p", f"e{i}m"))
+            done += [f"e{i}p", f"e{i}m"]
     table["U", 0] = (tuple(done), ())
     return table
 
@@ -205,17 +218,16 @@
     def unpack(c):
         low = lax.broadcasted_iota(jnp.int32, (128, 128), 1) < 64
         first = lax.broadcasted_iota(jnp.int32, (16, 128), 0) < 8
-
         def body(slot, carry):
             away = (slot + 1) // 2
             source = lax.rem(z + jnp.where(slot % 2 == 0, away, NZ - away), NZ)
             for yp in range(2):
                 m = source * 2 + yp
-                e = pieces[c, slot, 2 * yp, 0:128, :].astype(F32)
-                o = pieces[c, slot, 2 * yp + 1, 0:128, :].astype(F32)
+                e = pieces[c, slot, 2 * yp, 0:128, :]
+                o = pieces[c, slot, 2 * yp + 1, 0:128, :]
                 lanes = pl.ds(pl.multiple_of(m * 128, 128), 128)
-                xs[pl.ds(top_at, 128), lanes] = jnp.where(low, e, o).astype(BF16)
-                xs[pl.ds(bottom_at, 128), lanes] = pltpu.roll(jnp.where(low, o, e), 64, 1).astype(BF16)
+                xs[pl.ds(top_at, 128), lanes] = jnp.where(low, e, o)
+                xs[pl.ds(bottom_at, 128), lanes] = pltpu.roll(jnp.where(low, o, e), 64, 1)
                 te = pieces[c, slot, 2 * yp, 128:144, :].astype(F32)
                 to = pieces[c, slot, 2 * yp + 1, 128:144, :].astype(F32)
                 tails[m, :, pl.ds(top_at, 128)] = jnp.where(first, te, to)
@@ -238,14 +250,21 @@
             device_id=device(*to), device_id_type=MESH)
 
     def multiply(g):
-        n = g % THIRDS
-        if g < THIRDS:
+        n = lax.rem(g, THIRDS)
+
+        @pl.when(g < THIRDS)
+        def _():
             pltpu.make_async_copy(wbuf.at[n], wbuf.at[n], w_sem.at[n]).wait()
+
+        @pl.when(n == 0)
+        def _():
+            unpack(g // THIRDS)
+
         acc = jnp.dot(xs[:, 0:2048], wbuf[n, :, 0:128, :].reshape(2048, 768), preferred_element_type=F32)
         acc += jnp.dot(xs[:, 2048:2304], wbuf[n, :, 128:144, :].reshape(256, 768), preferred_element_type=F32)
         psend[g] = acc[128:256].astype(BF16)
         rs(g, "pair").start()
-        own[g % 6] = acc[0:128]
+        own[lax.rem(g, 6)] = acc[0:128]
 
     def block(shift):
         return pl.ds(pl.multiple_of(at_x(shift) * 32, 32), 32)
@@ -299,26 +318,58 @@
             out_d[2 * (c - 2), :, columns] = hidden[0:16]
             out_d[2 * (c - 2) + 1, :, columns] = hidden[16:32]
 
-    greeted, arrived = False, set()
-    for kind, number, index in ORDER:
-        if kind in ("MM", "R1", "R2", "R3"):
-            {"MM": multiply, "R1": reduce_1, "R2": reduce_2, "R3": reduce_3}[kind](number)
-            continue
+    arrived = set()
+
+    def perform(kind, number, index):
+        if kind in ("R1", "R2", "R3"):
+            {"R1": reduce_1, "R2": reduce_2, "R3": reduce_3}[kind](number)
+            return
         before, after = STEPS[number][kind, index]
         if kind == "pack":
             pack(number)
-            if not greeted:
-                pl.semaphore_wait(barrier, len(hops))
-                greeted = True
         for name in before:
             if (number, name) not in arrived:
                 copy(number, name).wait_recv()
                 arrived.add((number, name))
         for name in after:
             copy(number, name).start()
-        if kind == "U":
-            unpack(number)
-
+
+    between = [[]]
+    for kind, number, index in ORDER:
+        if kind == "MM":
+            between.append([])
+        else:
+            between[-1].append((kind, number, index))
+    pack(0)
+    pl.semaphore_wait(barrier, len(hops))
+    for name in STEPS[0]["pack", 0][1]:
+        copy(0, name).start()
+    between[0].remove(("pack", 0, 0))
+    for work in between[0]:
+        perform(*work)
+
+    def round_of(g, carry):
+        multiply(g)
+
+        def follow(lo, hi):
+            if hi - lo == 1:
+                for work in between[lo + 1]:
+                    perform(*work)
+                return
+            middle = (lo + hi) // 2
+
+            @pl.when(g < middle)
+            def _():
+                follow(lo, middle)
+
+            @pl.when(g >= middle)
+            def _():
+                follow(middle, hi)
+
+        follow(0, GROUPS)
+        return carry
+
+    lax.fori_loop(0, GROUPS, round_of, 0)
     for c in range(CHUNKS):
         for name in PLANS[c]:
             assert (c, name) in arrived

time: 79.5 us -> 70.3 us (0.88)
  Pallas kernels: 75.6 us -> 66.3 us
    pallas_call x1, Pallas kernels: 75.6 us -> 66.3 us  [shards(): pl.pallas_call(kernel, out_shape=(jax.ShapeDtypeStruct((64, 1152), BF16),...]
where the time goes in v3:
time: 70.3 us; the launch traced here: 70.1 us
  Pallas kernels  66.3 us (94%)
  local copies, waits for them, and re-layouts  3.16 us (4%)
    pallas_call x1, Pallas kernels, shards(): pl.pallas_call(kernel, out_shape=(jax.ShapeDtypeStruct((64, 1152), BF16),...  66.3 us
    unnamed x2, local copies, waits for them, and re-layouts  3.16 us

profile of v3, /device:TPU:1, one launch (start us, length us, event | category | flops | bytes accessed | tf_op | source)
XLA Modules:
  0.0 70.1 jit_solution(6778048703547393424)
XLA Ops:
  0.6 66.3 %shard_map.59 = (bf16[64,1152]{1,0:T(8,128)(2,1)}, bf16[4,16,1152]{2,1,0:T(8,128)(2,1)}) custom-call(bf16[72,512]{1,0:T(8,128)(2,1)} %bitcast.6, bf16[4,72,128]{2,1,0:T(8,128)(2,1)} %bitcast.7, bf16[16,144,1152]{2,1,0:T(8,128)(2,1)} %bitcast.4, bf16[16,144,1152]{2,1,0:T(8,128)(2,1)} %bitcast.5), custom_call_target="tpu_custom_call" | custom-call | flops 10871635968 | bytes 11000000 | tf_op jit(solution)/shard_map/pallas_call | solution.py:387
  67.0 1.6 %copy.8 = bf16[64,1152]{1,0:T(8,128)(2,1)} copy(bf16[64,1152]{1,0:T(8,128)(2,1)} %get-tuple-element.4) | data formatting | bytes 294912
  68.6 1.6 %copy.9 = bf16[4,16,1152]{2,1,0:T(8,128)(2,1)} copy(bf16[4,16,1152]{2,1,0:T(8,128)(2,1)} %get-tuple-element.5) | data formatting | bytes 294912

commit v4 on v3

--- a/solution.py
+++ b/solution.py
@@ -112,7 +112,7 @@
 STEPS = [steps(c) for c in range(CHUNKS)]
 
 
-def kernel(prompt, decode, gate, up, out_p, out_d, pieces, wbuf, xs, tails, own, psend, precv,
+def kernel(prompt, decode, gate, up, out, pieces, wbuf, xs, tails, own, psend, precv,
            s1_out, s1_in, s2_out, s2_in, ag_send, ag_recv, rs_send, rs_recv, w_sem):
     gx, gy = lax.axis_index("gx"), lax.axis_index("gy")
     x, core = gx // 2, gx % 2
@@ -313,10 +313,9 @@
         hidden = (jax.nn.silu(total[:, 0:384]) * total[:, 384:768]).astype(BF16)
         columns = pl.ds(384 * n, 384)
         if c < 2:
-            out_p[pl.ds(32 * c, 32), columns] = hidden
-        else:
-            out_d[2 * (c - 2), :, columns] = hidden[0:16]
-            out_d[2 * (c - 2) + 1, :, columns] = hidden[16:32]
+            out[0, pl.ds(32 * c, 32), columns] = hidden
+        else:
+            out[1, pl.ds(32 * (c - 2), 32), columns] = hidden
 
     arrived = set()
 
@@ -384,11 +383,11 @@
     up_weight = up_weight.reshape(16, 144, 1152)
     vmem = pl.BlockSpec(memory_space=pltpu.VMEM)
     anywhere = pl.BlockSpec(memory_space=pl.ANY)
-    return pl.pallas_call(
+    both = pl.pallas_call(
         kernel,
-        out_shape=(jax.ShapeDtypeStruct((64, 1152), BF16), jax.ShapeDtypeStruct((4, 16, 1152), BF16)),
+        out_shape=jax.ShapeDtypeStruct((2, 64, 1152), BF16),
         in_specs=[vmem, vmem, anywhere, anywhere],
-        out_specs=(vmem, vmem),
+        out_specs=vmem,
         scratch_shapes=[
             pltpu.VMEM((CHUNKS, NZ, NY, 144, 128), BF16),
             pltpu.VMEM((THIRDS, 16, 144, 768), BF16),
@@ -411,6 +410,7 @@
             collective_id=0, has_side_effects=True, vmem_limit_bytes=56 * 1024 * 1024),
         cost_estimate=pl.CostEstimate(flops=2 * 1024 * 2304 * 2304, bytes_accessed=11_000_000, transcendentals=147456),
     )(prompt_tokens.T, decode_tokens.transpose(0, 2, 1), gate_weight, up_weight)
+    return both[0], both[1].reshape(4, 16, 1152)
 
 
 def solution(mesh):

time: 70.3 us -> 68.9 us (0.980)
  local copies, waits for them, and re-layouts: 3.16 us -> 1.72 us
    unnamed x2 -> x0, local copies, waits for them, and re-layouts: 3.16 us -> none
    slice x0 -> x1, local copies, waits for them, and re-layouts: none -> 1.72 us  [shards(): return (both[0], both[1].reshape(4, 16, 1152))]
where the time goes in v4:
time: 68.9 us; the launch traced here: 68.7 us
  Pallas kernels  66.4 us (96%)
  local copies, waits for them, and re-layouts  1.72 us (2%)
    pallas_call x1, Pallas kernels, shards(): pl.pallas_call(kernel, out_shape=jax.ShapeDtypeStruct((2, 64, 1152), BF16...  66.4 us
    slice x1, local copies, waits for them, and re-layouts, shards(): return (both[0], both[1].reshape(4, 16, 1152))  1.72 us

profile of v4, /device:TPU:1, one launch (start us, length us, event | category | flops | bytes accessed | tf_op | source)
XLA Modules:
  0.0 68.7 jit_solution(6049967879787117914)
XLA Ops:
  0.6 66.4 %shard_map.59 = bf16[2,64,1152]{2,1,0:T(8,128)(2,1)} custom-call(bf16[72,512]{1,0:T(8,128)(2,1)} %bitcast.10, bf16[4,72,128]{2,1,0:T(8,128)(2,1)} %bitcast.11, bf16[16,144,1152]{2,1,0:T(8,128)(2,1)} %bitcast.8, bf16[16,144,1152]{2,1,0:T(8,128)(2,1)} %bitcast.9), custom_call_target="tpu_custom_call" | custom-call | flops 10871635968 | bytes 11000000 | tf_op jit(solution)/shard_map/pallas_call | solution.py:386
  67.0 1.7 %fusion = (bf16[1,64,1152]{2,1,0:T(8,128)(2,1)}, bf16[64,1152]{1,0:T(8,128)(2,1)}) fusion(bf16[2,64,1152]{2,1,0:T(8,128)(2,1)} %shard_map.59), kind=kLoop, calls=%fused_computation.1 | loop fusion | bytes 589824 | tf_op jit(solution)/shard_map/slice | solution.py:413

commit v5 on v4

--- a/solution.py
+++ b/solution.py
@@ -140,15 +140,6 @@
     for axis, shift in sorted(hops):
         pl.semaphore_signal(barrier, inc=1, device_id=device(axis, shift), device_id_type=MESH)
 
-    for n in range(THIRDS):
-        for half, source in enumerate((gate, up)):
-            for begin, rows, to in ((0, 64, 0), (80, 64, 64), (64, 16, 128)):
-                pltpu.make_async_copy(
-                    source.at[:, pl.ds(begin, rows), pl.ds(384 * n, 384)],
-                    wbuf.at[n, :, pl.ds(to, rows), pl.ds(384 * half, 384)],
-                    w_sem.at[n],
-                ).start()
-
     odd = y % 2
     nt = (((1,), (1,)), ((), ()))
 
@@ -260,8 +251,9 @@
         def _():
             unpack(g // THIRDS)
 
-        acc = jnp.dot(xs[:, 0:2048], wbuf[n, :, 0:128, :].reshape(2048, 768), preferred_element_type=F32)
-        acc += jnp.dot(xs[:, 2048:2304], wbuf[n, :, 128:144, :].reshape(256, 768), preferred_element_type=F32)
+        weights = jnp.concatenate(
+            [wbuf[n, :, 0:128, :].reshape(2048, 768), wbuf[n, :, 128:144, :].reshape(256, 768)], axis=0)
+        acc = jnp.dot(xs[...], weights, preferred_element_type=F32)
         psend[g] = acc[128:256].astype(BF16)
         rs(g, "pair").start()
         own[lax.rem(g, 6)] = acc[0:128]
@@ -343,6 +335,16 @@
     pl.semaphore_wait(barrier, len(hops))
     for name in STEPS[0]["pack", 0][1]:
         copy(0, name).start()
+
+    for n in range(THIRDS):
+        for half, source in enumerate((gate, up)):
+            for begin, rows, to in ((0, 64, 0), (80, 64, 64), (64, 16, 128)):
+                pltpu.make_async_copy(
+                    source.at[:, pl.ds(begin, rows), pl.ds(384 * n, 384)],
+                    wbuf.at[n, :, pl.ds(to, rows), pl.ds(384 * half, 384)],
+                    w_sem.at[n],
+                ).start()
+
     between[0].remove(("pack", 0, 0))
     for work in between[0]:
         perform(*work)

time: 68.9 us -> 68.8 us (level)
  no operation moved by 1% of the time
where the time goes in v5:
time: 68.8 us; the launch traced here: 68.7 us
  Pallas kernels  66.3 us (96%)
  local copies, waits for them, and re-layouts  1.72 us (2%)
    pallas_call x1, Pallas kernels, shards(): pl.pallas_call(kernel, out_shape=jax.ShapeDtypeStruct((2, 64, 1152), BF16...  66.3 us
    slice x1, local copies, waits for them, and re-layouts, shards(): return (both[0], both[1].reshape(4, 16, 1152))  1.72 us

profile of v5, /device:TPU:1, one launch (start us, length us, event | category | flops | bytes accessed | tf_op | source)
XLA Modules:
  0.0 68.7 jit_solution(4901415396358377943)
XLA Ops:
  0.6 66.3 %shard_map.59 = bf16[2,64,1152]{2,1,0:T(8,128)(2,1)} custom-call(bf16[72,512]{1,0:T(8,128)(2,1)} %bitcast.10, bf16[4,72,128]{2,1,0:T(8,128)(2,1)} %bitcast.11, bf16[16,144,1152]{2,1,0:T(8,128)(2,1)} %bitcast.8, bf16[16,144,1152]{2,1,0:T(8,128)(2,1)} %bitcast.9), custom_call_target="tpu_custom_call" | custom-call | flops 10871635968 | bytes 11000000 | tf_op jit(solution)/shard_map/pallas_call | solution.py:388
  67.0 1.7 %fusion = (bf16[1,64,1152]{2,1,0:T(8,128)(2,1)}, bf16[64,1152]{1,0:T(8,128)(2,1)}) fusion(bf16[2,64,1152]{2,1,0:T(8,128)(2,1)} %shard_map.59), kind=kLoop, calls=%fused_computation.1 | loop fusion | bytes 589824 | tf_op jit(solution)/shard_map/slice | solution.py:415
